TPU v7x, 512 devices: a whole 4x8x8 slice. The times are simulated.
512 devices in a mesh: src: 16 (over z, core), tm: 32 (over x, y).
Axes of the slice: x: 4, y: 8, z: 8, core: 2. Of those that a mesh axis runs over, the one named last changes fastest.
Arguments:
- greens: bfloat16 [65536, 12288], P('tm', 'src')
- pairs: int32 [16, 2], P('src'), may hold values from 0 to 15, as said below
- onsets: int32 [16], replicated, may hold values from 0 to 32767
Outputs:
- gram: float32 [16, 768, 768], P('src', 'tm')
Inputs may be any that keep to these rules, and one draw needn't show every extreme that they name: `pairs`: row s names the blocks s and (s - 1) mod 16, in either order.
All inputs are finite; a program needn't handle non-finite values.
Results may differ from a plain program's by a relative error of at most 0.0003.
Values may be sent and summed in bfloat16 or wider, within the bound.
A program may use at most 64 MiB of HBM per device.

v0:
```python
import jax
import jax.numpy as jnp
from jax import lax
from jax.sharding import Mesh
from jax.sharding import PartitionSpec as P

TM = ("tm_0", "tm_1")


def from_behind(value, axis, by):
    length = lax.axis_size(axis)
    return lax.ppermute(value, axis, [(i, (i + by) % length) for i in range(length)])


def over_axes(value, axes):
    for axis in axes:
        value = lax.psum(value, axis)
    return value


def cut_along(value, dim, length):
    lengths = value.shape
    tiles = value.reshape(*lengths[:dim], length, lengths[dim] // length, *lengths[dim + 1 :])
    return jnp.moveaxis(tiles, dim, 0)


def sent_and_summed(value, axis, dim):
    length = lax.axis_size(axis)
    tiles = lax.all_to_all(cut_along(value, dim, length), axis, 0, 0, tiled=True)
    return jnp.sum(tiles, axis=0)


def on_device(greens, pairs, onsets):
    rows_dev, width = greens.shape
    row_group = lax.axis_index(TM)
    row_start = row_group * rows_dev
    owner = lax.axis_index("src")
    lower = from_behind(greens, "src", 1)
    first = pairs[0, 0]
    second = pairs[0, 1]
    row_ids = row_start + jnp.arange(rows_dev, dtype=jnp.int32)
    left = jnp.where(first == owner, greens, lower)
    right = jnp.where(first == owner, lower, greens)
    left = jnp.where((row_ids >= onsets[first])[:, None], left, jnp.zeros_like(left))
    right = jnp.where((row_ids >= onsets[second])[:, None], right, jnp.zeros_like(right))
    left_f = left.astype(jnp.float32)
    right_f = right.astype(jnp.float32)
    norm_left, norm_right = (
        over_axes(jnp.sum(left_f * left_f, axis=0), TM),
        over_axes(jnp.sum(right_f * right_f, axis=0), TM),
    )
    arrival = jnp.maximum(onsets[first], onsets[second])
    silent = row_start + rows_dev <= arrival
    share = width // lax.axis_size(TM)
    piece = left
    mine = sent_and_summed(
        lax.cond(
            silent,
            lambda: jnp.zeros((share * lax.axis_size(TM), width), jnp.float32),
            lambda: lax.dot_general(
                piece, right, (((0,), (0,)), ((), ())), preferred_element_type=jnp.float32
            ),
        ),
        TM,
        0,
    )
    scale_rows = lax.dynamic_slice_in_dim(lax.rsqrt(norm_left + 1e-06), row_group * share, share, 0)
    scale_cols = lax.rsqrt(norm_right + 1e-06)
    normalized = mine * scale_rows[:, None] * scale_cols[None, :]
    return normalized[None]


def solution(mesh):
    split = Mesh(mesh.devices.reshape(mesh.shape["src"], 4, 8), ("src", "tm_0", "tm_1"))
    in_specs = (P(TM, "src"), P("src", None), P())
    out_specs = P("src", TM, None)
    return jax.shard_map(
        on_device, mesh=split, in_specs=in_specs, out_specs=out_specs, check_vma=False
    )
```

profile of v0, /device:TPU:194, one launch (start us, length us, event | category | flops | bytes accessed | tf_op | source)
XLA Modules:
  0.0 122.4 jit_solution(4111299855507646524)
XLA Ops:
  0.0 0.0 collective-permute-start
  0.0 1.3 %fusion.4 = (s32[1,1]{1,0:T(1,128)}, s32[1,1]{1,0:T(1,128)}) fusion(s32[1,2]{1,0:T(1,128)} %param.6), kind=kLoop, calls=%fused_computation.12 | loop fusion | bytes 16 | tf_op jit(solution)/shard_map/slice | solution.py:40
  6.0 1.4 %fusion.3 = (s32[1]{0:T(128)}, s32[1]{0:T(128)}) fusion(s32[16]{0:T(128)} %param.7, s32[]{:T(128)S(6)} %select_n.31, s32[]{:T(128)S(6)} %select_n.30), kind=kLoop, calls=%fused_computation.11 | loop fusion | bytes 24 | tf_op jit(solution)/shard_map/dynamic_slice | solution.py:52
  8.8 1.3 %fusion.1 = (pred[2048]{0:T(1024)(128)(4,1)S(1)}, pred[2048]{0:T(1024)(128)(4,1)S(1)}) fusion(s32[]{:T(128)} %bitcast.3, s32[]{:T(128)S(6)} %mul.46, s32[]{:T(128)} %bitcast.1), kind=kLoop, calls=%fused_computation.7 | loop fusion | flops 6144 | bytes 4108 | tf_op jit(solution)/shard_map/ge | solution.py:45
  10.1 26.8 %collective-permute-done = bf16[2048,768]{1,0:T(8,128)(2,1)S(1)} collective-permute-done((bf16[2048,768]{1,0:T(8,128)(2,1)}, bf16[2048,768]{1,0:T(8,128)(2,1)S(1)}, u32[]{:S(2)}, u32[]{:S(2)}) %collective-permute-start) | collective-permute-done | bytes 3145760 | tf_op jit(solution)/shard_map/ppermute | solution.py:12
  36.9 4.6 %multiply_reduce_fusion = (f32[768]{0:T(1024)S(1)}, bf16[2048,768]{1,0:T(8,128)(2,1)S(1)}, f32[768]{0:T(1024)S(1)}, bf16[2048,768]{1,0:T(8,128)(2,1)S(1)}) fusion(bf16[2048,768]{1,0:T(8,128)(2,1)S(1)} %collective-permute-done, bf16[2048,768]{1,0:T(8,128)(2,1)} %param.5, pred[]{:T(512)S(6)} %eq.4, pred[2048]{0:T(1024)(128)(4,1)S(1)} %get-tuple-element.28, ...), kind=kLoop, calls=%fused_computation | loop fusion | flops 15727104 | bytes 12593153 | tf_op jit(solution)/shard_map/reduce_sum | solution.py:50
  41.5 0.2 conditional.1
  41.6 0.2 broadcast.59
  41.7 0.0 copy-start
  41.7 1.4 %copy-done = f32[768,768]{1,0:T(8,128)} copy-done((f32[768,768]{1,0:T(8,128)}, f32[768,768]{1,0:T(8,128)S(1)}, u32[]{:S(2)}) %copy-start) | copy-done | bytes 2359320
  43.1 12.9 %all-to-all-start = ((f32[32,24,768]{2,1,0:T(8,128)}), f32[32,24,768]{2,1,0:T(8,128)S(1)}, u32[]{:S(2)}, u32[]{:S(2)}) async-start(f32[32,24,768]{2,1,0:T(8,128)} %bitcast.11), calls=%async_computation | async-start | bytes 4718592 | tf_op jit(solution)/shard_map/all_to_all | solution.py:29
  56.0 9.5 %all-reduce.1 = (f32[768]{0:T(1024)S(1)}, f32[768]{0:T(1024)S(1)}) all-reduce(f32[768]{0:T(1024)S(1)} %get-tuple-element.20, f32[768]{0:T(1024)S(1)} %get-tuple-element.22), channel_id=1, replica_groups=mesh['src'=16,'tm_0'=4,'tm_1'=8] {'tm_0'}, use_global_device_ids=true, to_apply=%region_7.8 | all-reduce | flops 1536 | bytes 12288 | tf_op jit(solution)/shard_map/psum | solution.py:17
  65.5 56.0 %all-reduce = (f32[768]{0:T(1024)S(1)}, f32[768]{0:T(1024)S(1)}) all-reduce(f32[768]{0:T(1024)S(1)} %get-tuple-element.16, f32[768]{0:T(1024)S(1)} %get-tuple-element.17), channel_id=1, replica_groups=mesh['src'=16,'tm_0'=4,'tm_1'=8] {'tm_1'}, use_global_device_ids=true, to_apply=%region_8.9 | all-reduce | flops 1536 | bytes 12288 | tf_op jit(solution)/shard_map/psum | solution.py:17
  121.5 0.1 dynamic_slice.13
  121.6 0.0 all-to-all-done
  121.6 0.1 reduce_sum.29
  121.7 0.7 fusion
  (2 shorter events, 0.0 us)
Async XLA Ops:
  0.0 36.9 %collective-permute-start = (bf16[2048,768]{1,0:T(8,128)(2,1)}, bf16[2048,768]{1,0:T(8,128)(2,1)S(1)}, u32[]{:S(2)}, u32[]{:S(2)}) collective-permute-start(bf16[2048,768]{1,0:T(8,128)(2,1)} %param.5), channel_id=1, source_target_pairs={{0,32},{32,64},{64,96},{96,128},{128,160},{160,192},{192,224},{224... | collective-permute-start | bytes 9437192 | tf_op jit(solution)/shard_map/ppermute | solution.py:12
  41.7 1.4 %copy-start = (f32[768,768]{1,0:T(8,128)}, f32[768,768]{1,0:T(8,128)S(1)}, u32[]{:S(2)}) copy-start(f32[768,768]{1,0:T(8,128)S(1)} %get-tuple-element.30) | copy-start | bytes 7077892
  43.1 78.5 %all-to-all-start = ((f32[32,24,768]{2,1,0:T(8,128)}), f32[32,24,768]{2,1,0:T(8,128)S(1)}, u32[]{:S(2)}, u32[]{:S(2)}) async-start(f32[32,24,768]{2,1,0:T(8,128)} %bitcast.11), calls=%async_computation | async-start | bytes 4718592 | tf_op jit(solution)/shard_map/all_to_all | solution.py:29
where the time goes:
time: 123 us; the launch traced here: 122 us
  blocking collectives  65.5 us (53%)
  waiting for transfers between devices  26.8 us (22%)
  starting transfers between devices  12.9 us (10%)
  other arithmetic  6.8 us (6%)
  between operations  6.13 us (5%)
  local copies, waits for them, and re-layouts  4.37 us (4%)
    psum x2, blocking collectives, over_axes(): value = lax.psum(value, axis)  65.5 us
    ppermute x1, waiting for transfers between devices, from_behind(): lax.ppermute(value, axis, [(i, (i + by) % length) for i in range(length)])  26.8 us
    all_to_all x1, starting transfers between devices, sent_and_summed(): lax.all_to_all(cut_along(value, dim, length), axis, 0, 0, tiled=True)  12.9 us
    reduce_sum x1, other arithmetic, on_device(): jnp.sum(right_f * right_f, axis=0)  4.62 us
  transfers between devices with their start and end apart: 2, of which 1 were waited for; matrix products, arithmetic and copies ran while one was open for 3% of the time, Pallas kernels for 0%

commit v1 on v0

v1 whole, which is shorter than its diff:
```python
import functools

import jax
import jax.numpy as jnp
from jax import lax
from jax.experimental import pallas as pl
from jax.experimental.pallas import tpu as pltpu
from jax.sharding import Mesh
from jax.sharding import PartitionSpec as P

MESH = pl.DeviceIdType.MESH
F32 = jnp.float32
BF16 = jnp.bfloat16
NZ, NX, NY = 8, 4, 8
LAG0 = 4
LAG1 = 1


def remote(src, dst, send, recv, **where):
    return pltpu.make_async_remote_copy(
        src_ref=src, dst_ref=dst, send_sem=send, recv_sem=recv, device_id=where, device_id_type=MESH
    )


def kernel(
    greens, pairs, onsets, out,
    held, nat, sent, got, shift, tbuf, nbuf, units, rx_half, rx_full, ry_half, ry_full,
    wide, w_half, w_full, res, res_c, npart, nx_got, ny_got, scale, flag, flag_c,
    load_sem, raw_send, raw_recv, z_send, z_recv, core_send, ring_send, ring_recv,
    res_send, res_recv, n_send, n_recv, f_send, f_recv,
):
    z, c, x, y = (lax.axis_index(a) for a in ("z", "c", "x", "y"))
    rows, width = greens.shape
    half = rows // 2
    cols = width // 3
    t = x * NY + y
    row_start = t * rows
    z_up, z_down = lax.rem(z + 1, NZ), lax.rem(z + NZ - 1, NZ)
    own = 2 * z + c
    low = lax.rem(own + 2 * NZ - 1, 2 * NZ)
    high = lax.rem(own + 1, 2 * NZ)

    def at_x(d):
        return lax.rem(x + d + NX, NX)

    def at_y(d):
        return lax.rem(y + d + NY, NY)

    bar = pltpu.get_barrier_semaphore()

    def hello(**where):
        pl.semaphore_signal(bar, inc=1, device_id=where, device_id_type=MESH)

    loads = [
        pltpu.make_async_copy(
            greens.at[pl.ds(i * 512, 512)], held.at[pl.ds(i * 512, 512)], load_sem.at[i]
        )
        for i in range(rows // 512)
    ]
    for i in (2, 3, 0, 1):
        pl.when(c == 0)(loads[i].start)
    for i in (0, 1, 2, 3):
        pl.when(c == 1)(loads[i].start)
    for d in range(1, NX):
        hello(x=at_x(d))
    for d in range(1, NY):
        hello(y=at_y(d))
    hello(c=1 - c)

    @pl.when(c == 0)
    def _():
        hello(z=z_up)
        hello(z=z_down)
        hello(z=z_down, c=1)

    @pl.when(c == 1)
    def _():
        hello(z=z_up, c=0)

    for k in range(3):
        i = lax.broadcasted_iota(jnp.int32, (cols, width), 0)
        j = lax.broadcasted_iota(jnp.int32, (cols, width), 1)
        hit = j == i + 16 * lax.shift_right_logical(i, 3) + 8 * k
        shift[k] = jnp.where(hit, F32(1), F32(0)).astype(BF16)

    own_first = pairs[0, 0] == own
    flag[...] = jnp.where(own_first, jnp.ones_like(flag), jnp.zeros_like(flag))

    @pl.when(c == 0)
    def _():
        pl.semaphore_wait(bar, 14)

    @pl.when(c == 1)
    def _():
        pl.semaphore_wait(bar, 12)

    def chunk(k, h):
        for b in range(2):
            part = held[pl.ds(h * half + b * 512, 512), :]
            sent[k, h, :, pl.ds(b * 512, 512)] = lax.dot_general(
                shift[k], part, (((1,), (1,)), ((), ())), preferred_element_type=F32
            ).astype(BF16)

    def masks(nat_rows, nat_onset):
        own_from = onsets[own] - row_start
        nat_from = nat_onset - row_start
        step = 64

        def body(i, total):
            at = pl.multiple_of(i * step, step)
            block = held[pl.ds(at, step), :].astype(F32)
            ids = at + lax.broadcasted_iota(jnp.int32, (step, width), 0)
            mine = jnp.where(ids >= own_from, block, F32(0))

            @pl.when(i < nat_rows // step)
            def _():
                nat[pl.ds(at, step), :] = jnp.where(ids >= nat_from, block, F32(0)).astype(BF16)

            return total + jnp.sum((mine * mine).reshape(step // 8, 8, width), axis=0)

        total = lax.fori_loop(0, rows // step, body, jnp.zeros((8, width), F32))
        npart[0] = jnp.sum(total, axis=0, keepdims=True)

    def mask_c():
        nat_from = jnp.maximum(onsets[high], onsets[lax.rem(own + 2, 2 * NZ)]) - row_start
        step = 64

        @pl.loop(0, half // step)
        def _(i):
            at = pl.multiple_of(half + i * step, step)
            ids = at + lax.broadcasted_iota(jnp.int32, (step, width), 0)
            block = nat[pl.ds(at, step), :].astype(F32)
            nat[pl.ds(at, step), :] = jnp.where(ids >= nat_from, block, F32(0)).astype(BF16)

    nx = [
        remote(npart.at[0], nx_got.at[d - 1], n_send.at[d - 1], n_recv.at[d - 1], x=at_x(d))
        for d in range(1, NX)
    ]
    ny = [
        remote(npart.at[1], ny_got.at[d - 1], n_send.at[2 + d], n_recv.at[2 + d], y=at_y(d))
        for d in range(1, NY)
    ]

    def norm_x():
        for cp in nx:
            cp.start()

    def norm_y():
        total = npart[0]
        for d, cp in enumerate(nx):
            cp.wait_recv()
            total = total + nx_got[d]
        npart[1] = total
        for cp in ny:
            cp.start()

    def norm_end(pass_on):
        total = npart[1]
        for d, cp in enumerate(ny):
            cp.wait_recv()
            total = total + ny_got[d]
        scale[0] = lax.rsqrt(total + F32(1e-6))
        pass_on.start()

    def product(u, k, parts, natural):
        for q in range(3):
            at = pl.ds(q * cols, cols)
            total = None
            for slot, first in parts:
                term = jnp.dot(got[k, slot], nat[pl.ds(first, half), at], preferred_element_type=F32)
                total = term if total is None else total + term
            tbuf[:, at] = total
            nbuf[at, :] = total.T
        for g in range(NX):
            turned = nbuf[pl.ds(192 * g, 192), :].reshape(8, 3, 8, cols)
            for q in range(3):
                at = pl.ds(q * cols, cols)
                plain = tbuf[pl.ds(64 * g, 64), at]
                units[u, g, :, at] = jnp.where(natural, turned[:, q].reshape(64, cols), plain)

    def ring(n, axis, to, group, add, halves, slots, sems, finish):
        deep = n // 2

        def sends(step, lo, hi):
            send, recv, base = sems
            return (
                remote(lo, slots(step, 0), send.at[base + 2 * step], recv.at[base + 2 * step], **{axis: to(1)}),
                remote(hi, slots(step, 1), send.at[base + 2 * step + 1], recv.at[base + 2 * step + 1], **{axis: to(-1)}),
            )

        started = []

        def begin():
            far = group(to(deep))
            pair = sends(0, halves(far, 0), halves(far, 1))
            started.append(pair)
            for cp in pair:
                cp.start()

        def middle(step):
            for side, cp in enumerate(started[-1]):
                cp.wait_recv()
                where = group(to((deep - step) * (1 - 2 * side)))
                add(where, slots(step - 1, side), side if step == 1 else None)
            pair = sends(step, group(to(deep - step)), group(to(step - deep)))
            started.append(pair)
            for cp in pair:
                cp.start()

        def end():
            for cp in started[-1]:
                cp.wait_recv()
            finish(group(to(0))[...] + slots(deep - 1, 0)[...] + slots(deep - 1, 1)[...])

        stages = [begin] + [functools.partial(middle, s) for s in range(1, deep)] + [end]
        return stages, started

    def add_into(halves):
        def add(where, arrived, side):
            where = where if side is None else halves(where, side)
            where[...] = where[...] + arrived[...]

        return add

    def unit_stages(u, x_first, done):
        sems = (ring_send, ring_recv)

        def put(value):
            wide[u, pl.ds(0, 64 if x_first else 32)] = value.reshape(-1, width)

        def put_res(value):
            res[u] = value
            done()

        def half_rows_x(ref, s):
            return ref.at[pl.ds(32 * s, 32)]

        def half_rows_y(ref, s):
            return ref.at[pl.ds(2 * s, 2)]

        def half_cols(ref, s):
            return ref.at[:, pl.ds(s * (width // 2), width // 2)]

        if x_first:
            v = u - 3
            one = ring(
                NX, "x", at_x, lambda g: units.at[u, g], add_into(half_rows_x), half_rows_x,
                lambda step, side: (rx_half.at[v, side] if step == 0 else rx_full.at[v, side]),
                (*sems, 12 * u), put,
            )
            n, axis, to, base = NY, "y", at_y, 12 * u + 4
        else:
            one = ring(
                NY, "y", at_y, lambda g: units.at[u, :, pl.ds(pl.multiple_of(8 * g, 8), 8)],
                add_into(half_rows_y), half_rows_y,
                lambda step, side: (ry_half.at[u, side] if step == 0 else ry_full.at[u, step - 1, side]),
                (*sems, 12 * u), put,
            )
            n, axis, to, base = NX, "x", at_x, 12 * u + 8
        two = ring(
            n, axis, to, lambda g: wide.at[u, pl.ds(pl.multiple_of(8 * g, 8), 8)], add_into(half_cols), half_cols,
            lambda step, side: (w_half.at[u, side] if step == 0 else w_full.at[u, step - 1, side]),
            (*sems, base), put_res,
        )
        a, b = one[0], two[0]

        def joint():
            a[-1]()
            b[0]()

        return a[:-1] + [joint] + b[1:], (one[1], two[1])

    def finish_tile(direct, turned):
        total = None
        for k in range(3):
            out[0, pl.ds(8 * k, 8), :] = direct(k)
            piece = turned(k)
            piece = jnp.concatenate([piece[:, q * cols : (q + 1) * cols] for q in range(3)], axis=0)
            top = piece.astype(BF16).astype(F32)
            rest = piece - top
            mid = rest.astype(BF16).astype(F32)
            stack = jnp.concatenate([top, mid, rest - mid], axis=0).astype(BF16)
            term = jnp.dot(stack, shift[k], preferred_element_type=F32)
            total = term if total is None else total + term
        value = out[0] + (total[:24] + total[24:48] + total[48:])
        mine, other = scale[0], scale[1]
        left = jnp.where(own_first, mine, other)
        right = jnp.where(own_first, other, mine)
        i = lax.broadcasted_iota(jnp.int32, (24, width), 0)
        j = lax.broadcasted_iota(jnp.int32, (24, width), 1)
        down = jnp.sum(jnp.where(j == i + 24 * t, left, F32(0)), axis=1, keepdims=True)
        out[0] = value * down * right

    def wait_sends(groups, others):
        for one, two in groups:
            for pair in one + two:
                for cp in pair:
                    cp.wait_send()
        for cp in nx + ny + others:
            cp.wait_send()

    raw = remote(greens.at[pl.ds(half, half)], nat.at[pl.ds(half, half)], raw_send, raw_recv, c=0)

    @pl.when(c == 0)
    def _():
        flags = remote(flag, flag_c, f_send, f_recv, z=z_down)
        flags.start()
        to_c = [remote(sent.at[k, 1], got.at[k, 1], z_send.at[k], z_recv.at[k, 1], z=z_down) for k in range(3)]
        to_a = [
            [remote(sent.at[k, h], got.at[k, h], core_send.at[k, h], z_recv.at[k, h], c=1) for h in range(2)]
            for k in range(3)
        ]
        for i in (2, 3):
            loads[i].wait()
        for k in range(3):
            chunk(k, 1)
            to_c[k].start()
            to_a[k][1].start()
            if k == 0:
                for i in (0, 1):
                    loads[i].wait()
            chunk(k, 0)
            to_a[k][0].start()
        masks(half, jnp.maximum(onsets[own], onsets[low]))
        norm_x()
        raw.wait_recv()
        mask_c()
        passed = remote(scale.at[0], scale.at[1], n_send.at[10], n_recv.at[10], c=1)
        flags.wait_recv()
        natural_c = jnp.broadcast_to(flag_c[0:1, 0:1] < F32(0.5), (64, cols))
        res_out = [remote(res.at[3 + k], res_c.at[k], res_send.at[k], res_recv.at[k], z=z_up) for k in range(3)]

        def nothing():
            pass

        plan = []
        groups = []
        for k in range(3):
            stages, started = unit_stages(k, False, nothing)
            plan.append((LAG0 * k, k, 0, stages))
            groups.append(started)
            stages, started = unit_stages(3 + k, True, res_out[k].start)
            plan.append((LAG0 * k, k, 1, stages))
            groups.append(started)
        for slot in range(2 * LAG0 + 7):
            for start, k, kind, stages in plan:
                if start == slot:
                    if kind == 0:
                        pltpu.make_async_copy(got.at[k, 0], got.at[k, 0], z_recv.at[k, 0]).wait()
                        product(k, k, ((0, 0),), own_first)
                    else:
                        pltpu.make_async_copy(got.at[k, 1], got.at[k, 1], z_recv.at[k, 1]).wait()
                        product(3 + k, k, ((1, half),), natural_c)
                if 0 <= slot - start < 7:
                    stages[slot - start]()
            if slot == 0:
                norm_y()
            if slot == 2:
                norm_end(passed)
        pltpu.make_async_copy(scale.at[1], scale.at[1], n_recv.at[10]).wait()
        for cp in res_out:
            cp.wait_recv()
        finish_tile(
            lambda k: jnp.where(own_first, res_c[k], res[k]), lambda k: jnp.where(own_first, res[k], res_c[k])
        )
        wait_sends(groups, [flags, passed] + to_c + to_a[0] + to_a[1] + to_a[2] + res_out)

    @pl.when(c == 1)
    def _():
        raw.start()
        to_b = [remote(sent.at[k, 0], got.at[k, 0], z_send.at[k], z_recv.at[k, 0], z=z_up, c=0) for k in range(3)]
        for i in (0, 1):
            loads[i].wait()
        for k in range(3):
            chunk(k, 0)
            to_b[k].start()
        for i in (2, 3):
            loads[i].wait()
        masks(rows, jnp.maximum(onsets[own], onsets[low]))
        norm_x()
        passed = remote(scale.at[0], scale.at[1], n_send.at[10], n_recv.at[10], z=z_up, c=0)

        def nothing():
            pass

        plan = []
        groups = []
        for k in range(3):
            stages, started = unit_stages(3 + k, True, nothing)
            plan.append((LAG1 * k, k, stages))
            groups.append(started)
        for slot in range(2 * LAG1 + 7):
            for start, k, stages in plan:
                if start == slot:
                    for h in range(2):
                        pltpu.make_async_copy(got.at[k, h], got.at[k, h], z_recv.at[k, h]).wait()
                    product(3 + k, k, ((0, 0), (1, half)), own_first)
                if 0 <= slot - start < 7:
                    stages[slot - start]()
            if slot == 1:
                norm_y()
            if slot == 3:
                norm_end(passed)
        pltpu.make_async_copy(scale.at[1], scale.at[1], n_recv.at[10]).wait()
        finish_tile(
            lambda k: jnp.where(own_first, F32(0), res[3 + k]), lambda k: jnp.where(own_first, res[3 + k], F32(0))
        )
        wait_sends(groups, [raw, passed] + to_b)


def on_device(greens, pairs, onsets):
    rows, width = greens.shape
    half, cols = rows // 2, width // 3
    vmem = pltpu.VMEM
    dma = pltpu.SemaphoreType.DMA
    return pl.pallas_call(
        kernel,
        out_shape=jax.ShapeDtypeStruct((1, width // (NX * NY), width), F32),
        in_specs=[
            pl.BlockSpec(memory_space=pl.ANY),
            pl.BlockSpec(memory_space=pltpu.SMEM),
            pl.BlockSpec(memory_space=pltpu.SMEM),
        ],
        out_specs=pl.BlockSpec(memory_space=vmem),
        scratch_shapes=[
            vmem((rows, width), BF16),
            vmem((rows, width), BF16),
            vmem((3, 2, cols, half), BF16),
            vmem((3, 2, cols, half), BF16),
            vmem((3, cols, width), BF16),
            vmem((cols, width), F32),
            vmem((width, cols), F32),
            vmem((6, NX, 64, width), F32),
            vmem((3, 2, 32, width), F32),
            vmem((3, 2, 64, width), F32),
            vmem((3, 2, 2, 8, width), F32),
            vmem((3, 3, 2, 4, 8, width), F32),
            vmem((6, 64, width), F32),
            vmem((6, 2, 8, width // 2), F32),
            vmem((6, 3, 2, 8, width), F32),
            vmem((6, 8, width), F32),
            vmem((3, 8, width), F32),
            vmem((2, 1, width), F32),
            vmem((NX - 1, 1, width), F32),
            vmem((NY - 1, 1, width), F32),
            vmem((2, 1, width), F32),
            vmem((8, 128), F32),
            vmem((8, 128), F32),
            dma((4,)),
            dma,
            dma,
            dma((3,)),
            dma((3, 2)),
            dma((3, 2)),
            dma((72,)),
            dma((72,)),
            dma((3,)),
            dma((3,)),
            dma((11,)),
            dma((11,)),
            dma,
            dma,
        ],
        compiler_params=pltpu.CompilerParams(
            collective_id=0, has_side_effects=True, vmem_limit_bytes=56 * 1024 * 1024
        ),
        cost_estimate=pl.CostEstimate(flops=5_000_000_000, bytes_accessed=4_000_000, transcendentals=768),
    )(greens, pairs, onsets)


def solution(mesh):
    split = Mesh(mesh.devices.reshape(NZ, 2, NX, NY), ("z", "c", "x", "y"))
    in_specs = (P(("x", "y"), ("z", "c")), P(("z", "c"), None), P())
    out_specs = P(("z", "c"), ("x", "y"), None)
    return jax.shard_map(on_device, mesh=split, in_specs=in_specs, out_specs=out_specs, check_vma=False)
```

time: 123 us -> 94 us (0.76)
  the two profiles are of different devices: /device:TPU:194 before, /device:TPU:2 now
where the time goes in v1:
time: 94 us; the launch traced here: 93.8 us
  Pallas kernels  92.3 us (98%)
  local copies, waits for them, and re-layouts  1.52 us (2%)
    pallas_call x1, Pallas kernels, on_device(): pl.pallas_call(kernel, out_shape=jax.ShapeDtypeStruct((1, width // (NX *...  92.3 us

profile of v1, /device:TPU:2, one launch (start us, length us, event | category | flops | bytes accessed | tf_op | source)
XLA Modules:
  0.0 93.8 jit_solution(13152183577850567596)
XLA Ops:
  0.0 92.3 %shard_map.37 = f32[1,24,768]{2,1,0:T(8,128)} custom-call(bf16[2048,768]{1,0:T(8,128)(2,1)} %greens.1, s32[1,2]{1,0:T(1,128)} %pairs.1, s32[16]{0:T(128)} %onsets.1), custom_call_target="tpu_custom_call" | custom-call | flops 5000000000 | bytes 4000000 | tf_op jit(solution)/shard_map/pallas_call | solution.py:416
  92.3 1.5 %copy.5 = f32[1,24,768]{2,1,0:T(8,128)} copy(f32[1,24,768]{2,1,0:T(8,128)} %shard_map.37) | data formatting | bytes 147456

commit v2 on v1

v2 whole, which is shorter than its diff:
```python
import functools

import jax
import jax.numpy as jnp
from jax import lax
from jax.experimental import pallas as pl
from jax.experimental.pallas import tpu as pltpu
from jax.sharding import Mesh
from jax.sharding import PartitionSpec as P

MESH = pl.DeviceIdType.MESH
F32 = jnp.float32
BF16 = jnp.bfloat16
NZ, NX, NY = 8, 4, 8


def remote(src, dst, send, recv, **where):
    return pltpu.make_async_remote_copy(
        src_ref=src, dst_ref=dst, send_sem=send, recv_sem=recv, device_id=where, device_id_type=MESH
    )


def kernel(
    greens, pairs, onsets, out,
    held, nat, nat_c, sent, got, got_c, shift, tbuf, nbuf, units, rx_got, ry_half, ry_full,
    wide, w_got, res, npart, nx_got, ny_got, scale, flag, flag_c,
    load_sem, z_send, z_recv, core_send, a_recv, sum_send, sum_recv, own_recv,
    n_send, n_recv, f_send, f_recv,
):
    z, c, x, y = (lax.axis_index(a) for a in ("z", "c", "x", "y"))
    rows, width = greens.shape
    half = rows // 2
    cols = width // 3
    t = x * NY + y
    row_start = t * rows
    z_up, z_down = lax.rem(z + 1, NZ), lax.rem(z + NZ - 1, NZ)
    own = 2 * z + c
    low = lax.rem(own + 2 * NZ - 1, 2 * NZ)
    high = lax.rem(own + 1, 2 * NZ)

    def at_x(d):
        return lax.rem(x + d + NX, NX)

    def at_y(d):
        return lax.rem(y + d + NY, NY)

    bar = pltpu.get_barrier_semaphore()

    def hello(**where):
        pl.semaphore_signal(bar, inc=1, device_id=where, device_id_type=MESH)

    loads = [
        pltpu.make_async_copy(
            greens.at[pl.ds(i * 512, 512)], held.at[pl.ds(i * 512, 512)], load_sem.at[i]
        )
        for i in range(rows // 512)
    ]
    for i in (2, 3, 0, 1):
        pl.when(c == 0)(loads[i].start)
    for i in (0, 1, 2, 3):
        pl.when(c == 1)(loads[i].start)
    hello(c=1 - c)

    @pl.when(c == 0)
    def _():
        hello(z=z_down, c=1)
        for d in range(NY):
            if d:
                hello(z=z_down, y=at_y(d), c=1)

    @pl.when(c == 1)
    def _():
        hello(z=z_up, c=0)
        for d in range(NY):
            if d:
                hello(z=z_up, y=at_y(d), c=0)

    for d in range(1, NX):
        hello(x=at_x(d))
    for d in range(1, NY):
        hello(y=at_y(d))

    for k in range(3):
        i = lax.broadcasted_iota(jnp.int32, (cols, width), 0)
        j = lax.broadcasted_iota(jnp.int32, (cols, width), 1)
        hit = j == i + 16 * lax.shift_right_logical(i, 3) + 8 * k
        shift[k] = jnp.where(hit, F32(1), F32(0)).astype(BF16)

    own_first = pairs[0, 0] == own
    flag[...] = jnp.where(own_first, jnp.ones_like(flag), jnp.zeros_like(flag))

    def chunk(k, h):
        for b in range(2):
            part = held[pl.ds(h * half + b * 512, 512), :]
            sent[k, h, :, pl.ds(b * 512, 512)] = lax.dot_general(
                shift[k], part, (((1,), (1,)), ((), ())), preferred_element_type=F32
            ).astype(BF16)

    def masks(first, last, targets, total):
        own_from = onsets[own] - row_start
        step = 64

        def body(i, total):
            at = pl.multiple_of(i * step, step)
            block = held[pl.ds(at, step), :].astype(F32)
            ids = at + lax.broadcasted_iota(jnp.int32, (step, width), 0)
            for ref, shifted, onset in targets:
                to = pl.multiple_of(at - shifted, step)
                ref[pl.ds(to, step), :] = jnp.where(ids >= onset - row_start, block, F32(0)).astype(BF16)
            mine = jnp.where(ids >= own_from, block, F32(0))
            return total + jnp.sum((mine * mine).reshape(step // 8, 8, width), axis=0)

        return lax.fori_loop(first // step, last // step, body, total)

    nx = [
        remote(npart.at[0], nx_got.at[d - 1], n_send.at[d - 1], n_recv.at[d - 1], x=at_x(d))
        for d in range(1, NX)
    ]
    ny = [
        remote(npart.at[1], ny_got.at[d - 1], n_send.at[2 + d], n_recv.at[2 + d], y=at_y(d))
        for d in range(1, NY)
    ]

    def norm_x(total):
        npart[0] = jnp.sum(total, axis=0, keepdims=True)
        for cp in nx:
            cp.start()

    def norm_y():
        total = npart[0]
        for d, cp in enumerate(nx):
            cp.wait_recv()
            total = total + nx_got[d]
        npart[1] = total
        for cp in ny:
            cp.start()

    def norm_end(pass_on):
        total = npart[1]
        for d, cp in enumerate(ny):
            cp.wait_recv()
            total = total + ny_got[d]
        scale[0] = lax.rsqrt(total + F32(1e-6))
        pass_on.start()

    def product(u, parts, natural):
        for q in range(3):
            at = pl.ds(q * cols, cols)
            total = None
            for moved, still in parts:
                term = jnp.dot(moved[...], still[:, at], preferred_element_type=F32)
                total = term if total is None else total + term
            tbuf[:, at] = total
            nbuf[at, :] = total.T
        for g in range(NX):
            turned = nbuf[pl.ds(192 * g, 192), :].reshape(8, 3, 8, cols)
            for q in range(3):
                at = pl.ds(q * cols, cols)
                plain = tbuf[pl.ds(64 * g, 64), at]
                units[u, g, :, at] = jnp.where(natural, turned[:, q].reshape(64, cols), plain)

    def arrived(ref, sem):
        pltpu.make_async_copy(ref, ref, sem).wait()

    class Early:
        def __init__(self, k):
            self.k, self.sends = k, []
            self.base = 12 * k

        def group(self, g):
            return units.at[self.k, :, pl.ds(pl.multiple_of(8 * g, 8), 8)]

        def slot(self, step, side):
            return ry_half.at[self.k, side] if step == 0 else ry_full.at[self.k, step - 1, side]

        def out(self, step, srcs):
            for side in range(2):
                at = self.base + 2 * step + side
                cp = remote(
                    srcs[side], self.slot(step, side), sum_send.at[at], sum_recv.at[at], y=at_y(1 - 2 * side)
                )
                cp.start()
                self.sends.append(cp)

        def begin(self):
            far = self.group(at_y(NY // 2))
            self.out(0, [far.at[pl.ds(2 * side, 2)] for side in range(2)])

        def middle(self, step):
            last = self.sends[-2:]
            for side in range(2):
                last[side].wait_recv()
                where = self.group(at_y((NY // 2 - step) * (1 - 2 * side)))
                if step == 1:
                    where = where.at[pl.ds(2 * side, 2)]
                where[...] = where[...] + self.slot(step - 1, side)[...]
            self.out(step, [self.group(at_y((NY // 2 - step) * (1 - 2 * side))) for side in range(2)])

        def across(self):
            for cp in self.sends[-2:]:
                cp.wait_recv()
            deep = NY // 2 - 1
            wide[self.k, pl.ds(0, 4)] = self.group(y)[...] + self.slot(deep, 0)[...] + self.slot(deep, 1)[...]
            for d in range(1, NX):
                at = self.base + 7 + d
                cp = remote(
                    wide.at[self.k, at_x(d)], w_got.at[self.k, d], sum_send.at[at], sum_recv.at[at], x=at_x(d)
                )
                cp.start()
                self.sends.append(cp)

        def end(self):
            total = wide[self.k, x]
            for d in range(1, NX):
                self.sends[-NX + d].wait_recv()
                total = total + w_got[self.k, d]
            res[self.k] = total

    class Late:
        def __init__(self, k, away):
            self.k, self.u, self.away, self.sends = k, 3 + k, away, []
            self.base = 12 * self.u

        def begin(self):
            for d in (2, 1, 3):
                at = self.base + d
                cp = remote(
                    units.at[self.u, at_x(d)], rx_got.at[self.k, d - 1], sum_send.at[at], sum_recv.at[at], x=at_x(d)
                )
                cp.start()
                self.sends.append(cp)

        def across(self):
            total = units[self.u, x]
            for i, d in enumerate((2, 1, 3)):
                self.sends[i].wait_recv()
                total = total + rx_got[self.k, d - 1]
            wide[self.u] = total.reshape(8, 8, width)
            for d in (4, 3, 5, 2, 6, 1, 7, 0):
                at = self.base + 4 + d
                if self.away:
                    cp = remote(
                        wide.at[self.u, at_y(d)], w_got.at[self.k, d], sum_send.at[at], own_recv.at[8 * self.k + d],
                        z=z_up, c=0, y=at_y(d),
                    )
                elif d:
                    cp = remote(
                        wide.at[self.u, at_y(d)], w_got.at[self.u, d], sum_send.at[at], sum_recv.at[at], y=at_y(d)
                    )
                else:
                    continue
                cp.start()
                self.sends.append(cp)

        def end(self):
            total = wide[self.u, y]
            for i, d in enumerate((4, 3, 5, 2, 6, 1, 7)):
                self.sends[3 + i].wait_recv()
                total = total + w_got[self.u, d]
            res[self.u] = total

    def end_c(k):
        total = None
        for d in range(NY):
            arrived(w_got.at[k, d], own_recv.at[8 * k + d])
            total = w_got[k, d] if total is None else total + w_got[k, d]
        res[k] = total

    def finish_tile(direct, turned):
        total = None
        for k in range(3):
            out[0, pl.ds(8 * k, 8), :] = direct(k)
            piece = turned(k)
            piece = jnp.concatenate([piece[:, q * cols : (q + 1) * cols] for q in range(3)], axis=0)
            top = piece.astype(BF16).astype(F32)
            rest = piece - top
            mid = rest.astype(BF16).astype(F32)
            stack = jnp.concatenate([top, mid, rest - mid], axis=0).astype(BF16)
            term = jnp.dot(stack, shift[k], preferred_element_type=F32)
            total = term if total is None else total + term
        value = out[0] + (total[:24] + total[24:48] + total[48:])
        mine, other = scale[0], scale[1]
        left = jnp.where(own_first, mine, other)
        right = jnp.where(own_first, other, mine)
        i = lax.broadcasted_iota(jnp.int32, (24, width), 0)
        j = lax.broadcasted_iota(jnp.int32, (24, width), 1)
        down = jnp.sum(jnp.where(j == i + 24 * t, left, F32(0)), axis=1, keepdims=True)
        out[0] = value * down * right

    def wait_sends(*groups):
        for group in groups:
            for cp in group:
                cp.wait_send()

    nothing = jnp.zeros((8, width), F32)
    first_rows, last_rows = pl.ds(0, half), pl.ds(half, half)

    @pl.when(c == 0)
    def _():
        flags = remote(flag, flag_c, f_send, f_recv, z=z_down, c=1)
        to_c = [remote(sent.at[k, 1], got_c.at[k], z_send.at[k], z_recv.at[k], z=z_down, c=1) for k in range(3)]
        to_a = [
            [remote(sent.at[k, h], got.at[k, h], core_send.at[k, h], a_recv.at[k, h], c=1) for h in range(2)]
            for k in range(3)
        ]
        passed = remote(scale.at[0], scale.at[1], n_send.at[10], n_recv.at[10], c=1)
        for i in (2, 3):
            loads[i].wait()
        chunk(0, 1)
        pl.semaphore_wait(bar, NX + NY - 1 + NY)
        to_c[0].start()
        to_a[0][1].start()
        flags.start()
        for i in (0, 1):
            loads[i].wait()
        for k in range(3):
            if k:
                chunk(k, 1)
                to_c[k].start()
                to_a[k][1].start()
            chunk(k, 0)
            to_a[k][0].start()
        total = masks(0, half, [(nat, 0, jnp.maximum(onsets[own], onsets[low]))], nothing)
        norm_x(masks(half, rows, [], total))

        tiles = [Late(k, False) for k in range(3)]

        def make(k):
            arrived(got.at[k, 0], z_recv.at[k])
            product(3 + k, ((got.at[k, 0], nat.at[first_rows]),), own_first)
            tiles[k].begin()

        make(0)
        norm_y()
        make(1)
        tiles[0].across()
        norm_end(passed)
        make(2)
        tiles[1].across()
        tiles[0].end()
        end_c(0)
        tiles[2].across()
        tiles[1].end()
        end_c(1)
        tiles[2].end()
        end_c(2)
        arrived(scale.at[1], n_recv.at[10])
        finish_tile(
            lambda k: jnp.where(own_first, res[k], res[3 + k]), lambda k: jnp.where(own_first, res[3 + k], res[k])
        )
        wait_sends([flags, passed], to_c, nx, ny, *to_a, *(tile.sends for tile in tiles))

    @pl.when(c == 1)
    def _():
        to_b = [remote(sent.at[k, 0], got.at[k, 0], z_send.at[k], z_recv.at[k], z=z_up, c=0) for k in range(3)]
        passed = remote(scale.at[0], scale.at[1], n_send.at[10], n_recv.at[10], z=z_up, c=0)
        for i in (0, 1):
            loads[i].wait()
        chunk(0, 0)
        pl.semaphore_wait(bar, NX + NY - 1 + NY)
        to_b[0].start()
        for k in (1, 2):
            chunk(k, 0)
            to_b[k].start()
        for i in (2, 3):
            loads[i].wait()
        onset_a = jnp.maximum(onsets[own], onsets[low])
        onset_c = jnp.maximum(onsets[own], onsets[high])
        total = masks(0, half, [(nat, 0, onset_a)], nothing)
        norm_x(masks(half, rows, [(nat, 0, onset_a), (nat_c, half, onset_c)], total))

        early = [Early(k) for k in range(3)]
        late = [Late(k, True) for k in range(3)]

        def make_a(k):
            for h in range(2):
                arrived(got.at[k, h], a_recv.at[k, h])
            product(k, ((got.at[k, 0], nat.at[first_rows]), (got.at[k, 1], nat.at[last_rows])), own_first)
            early[k].begin()

        def make_c(k):
            if k == 0:
                arrived(flag_c, f_recv)
            arrived(got_c.at[k], z_recv.at[k])
            natural = jnp.broadcast_to(flag_c[0:1, 0:1] < F32(0.5), (64, cols))
            product(3 + k, ((got_c.at[k], nat_c),), natural)
            late[k].begin()

        for k in range(3):
            make_a(k)
        make_c(0)
        norm_y()
        for k in range(3):
            early[k].middle(1)
        make_c(1)
        late[0].across()
        norm_end(passed)
        for k in range(3):
            early[k].middle(2)
        make_c(2)
        late[1].across()
        for k in range(3):
            early[k].middle(3)
        late[2].across()
        for k in range(3):
            early[k].across()
        for k in range(3):
            early[k].end()
        arrived(scale.at[1], n_recv.at[10])
        finish_tile(
            lambda k: jnp.where(own_first, F32(0), res[k]), lambda k: jnp.where(own_first, res[k], F32(0))
        )
        wait_sends([passed], to_b, nx, ny, *(tile.sends for tile in early + late))


def on_device(greens, pairs, onsets):
    rows, width = greens.shape
    half, cols = rows // 2, width // 3
    vmem = pltpu.VMEM
    dma = pltpu.SemaphoreType.DMA
    return pl.pallas_call(
        kernel,
        out_shape=jax.ShapeDtypeStruct((1, width // (NX * NY), width), F32),
        in_specs=[
            pl.BlockSpec(memory_space=pl.ANY),
            pl.BlockSpec(memory_space=pltpu.SMEM),
            pl.BlockSpec(memory_space=pltpu.SMEM),
        ],
        out_specs=pl.BlockSpec(memory_space=vmem),
        scratch_shapes=[
            vmem((rows, width), BF16),
            vmem((rows, width), BF16),
            vmem((half, width), BF16),
            vmem((3, 2, cols, half), BF16),
            vmem((3, 2, cols, half), BF16),
            vmem((3, cols, half), BF16),
            vmem((3, cols, width), BF16),
            vmem((cols, width), F32),
            vmem((width, cols), F32),
            vmem((6, NX, 64, width), F32),
            vmem((3, NX - 1, 64, width), F32),
            vmem((3, 2, 2, 8, width), F32),
            vmem((3, 3, 2, 4, 8, width), F32),
            vmem((6, 8, 8, width), F32),
            vmem((6, 8, 8, width), F32),
            vmem((6, 8, width), F32),
            vmem((2, 1, width), F32),
            vmem((NX - 1, 1, width), F32),
            vmem((NY - 1, 1, width), F32),
            vmem((2, 1, width), F32),
            vmem((8, 128), F32),
            vmem((8, 128), F32),
            dma((4,)),
            dma((3,)),
            dma((3,)),
            dma((3, 2)),
            dma((3, 2)),
            dma((72,)),
            dma((72,)),
            dma((24,)),
            dma((11,)),
            dma((11,)),
            dma,
            dma,
        ],
        compiler_params=pltpu.CompilerParams(
            collective_id=0, has_side_effects=True, vmem_limit_bytes=56 * 1024 * 1024
        ),
        cost_estimate=pl.CostEstimate(flops=5_000_000_000, bytes_accessed=4_000_000, transcendentals=768),
    )(greens, pairs, onsets)


def solution(mesh):
    split = Mesh(mesh.devices.reshape(NZ, 2, NX, NY), ("z", "c", "x", "y"))
    in_specs = (P(("x", "y"), ("z", "c")), P(("z", "c"), None), P())
    out_specs = P(("z", "c"), ("x", "y"), None)
    return jax.shard_map(on_device, mesh=split, in_specs=in_specs, out_specs=out_specs, check_vma=False)
```

time: 94 us -> 64.1 us (0.68)
  the two profiles are of different devices: /device:TPU:2 before, /device:TPU:8 now
where the time goes in v2:
time: 64.1 us; the launch traced here: 64 us
  Pallas kernels  62.4 us (97%)
  local copies, waits for them, and re-layouts  1.52 us (2%)
    pallas_call x1, Pallas kernels, on_device(): pl.pallas_call(kernel, out_shape=jax.ShapeDtypeStruct((1, width // (NX *...  62.4 us
    unnamed x1, local copies, waits for them, and re-layouts  1.52 us

profile of v2, /device:TPU:8, one launch (start us, length us, event | category | flops | bytes accessed | tf_op | source)
XLA Modules:
  0.0 64.0 jit_solution(17528154874903108262)
XLA Ops:
  0.0 62.4 %shard_map.37 = f32[1,24,768]{2,1,0:T(8,128)} custom-call(bf16[2048,768]{1,0:T(8,128)(2,1)} %greens.1, s32[1,2]{1,0:T(1,128)} %pairs.1, s32[16]{0:T(128)} %onsets.1), custom_call_target="tpu_custom_call" | custom-call | flops 5000000000 | bytes 4000000 | tf_op jit(solution)/shard_map/pallas_call | solution.py:421
  62.4 1.5 %copy.5 = f32[1,24,768]{2,1,0:T(8,128)} copy(f32[1,24,768]{2,1,0:T(8,128)} %shard_map.37) | data formatting | bytes 147456

commit v3 on v2

--- a/solution.py
+++ b/solution.py
@@ -12,6 +12,7 @@
 F32 = jnp.float32
 BF16 = jnp.bfloat16
 NZ, NX, NY = 8, 4, 8
+FAR_FIRST = (4, 3, 5, 2, 6, 1, 7)
 
 
 def remote(src, dst, send, recv, **where):
@@ -23,7 +24,7 @@
 def kernel(
     greens, pairs, onsets, out,
     held, nat, nat_c, sent, got, got_c, shift, tbuf, nbuf, units, rx_got, ry_half, ry_full,
-    wide, w_got, res, npart, nx_got, ny_got, scale, flag, flag_c,
+    wide, w_got, res, both, npart, nx_got, ny_got, scale, flag, flag_c,
     load_sem, z_send, z_recv, core_send, a_recv, sum_send, sum_recv, own_recv,
     n_send, n_recv, f_send, f_recv,
 ):
@@ -83,7 +84,11 @@
     for k in range(3):
         i = lax.broadcasted_iota(jnp.int32, (cols, width), 0)
         j = lax.broadcasted_iota(jnp.int32, (cols, width), 1)
-        hit = j == i + 16 * lax.shift_right_logical(i, 3) + 8 * k
+        if k < 2:
+            hit = j == i + 16 * lax.shift_right_logical(i, 3) + 8 * k
+        else:
+            h, rest = lax.shift_right_logical(i, 7), i & 127
+            hit = j == rest + 20 * lax.shift_right_logical(rest, 2) + 16 + 4 * h
         shift[k] = jnp.where(hit, F32(1), F32(0)).astype(BF16)
 
     own_first = pairs[0, 0] == own
@@ -159,146 +164,185 @@
                 plain = tbuf[pl.ds(64 * g, 64), at]
                 units[u, g, :, at] = jnp.where(natural, turned[:, q].reshape(64, cols), plain)
 
+    def product_half(u, h, parts, natural):
+        total = None
+        for moved, still in parts:
+            term = jnp.dot(moved[...], still[...], preferred_element_type=F32)
+            total = term if total is None else total + term
+        half_cols, few = width // 2, cols // 2
+        nbuf[:, pl.ds(0, few)] = total.T
+        left, right = total[:, :half_cols], total[:, half_cols:]
+        top = lax.broadcasted_iota(jnp.int32, (few, half_cols), 0) & 7 < 4
+        even = jnp.where(top, left, pltpu.roll(right, 4, 0)).reshape(16, 1, 8, half_cols)
+        odd = jnp.where(top, pltpu.roll(left, few - 4, 0), right).reshape(16, 1, 8, half_cols)
+        tbuf[:, pl.ds(0, half_cols)] = jnp.concatenate([even, odd], axis=1).reshape(cols, half_cols)
+        for g in range(NX):
+            turned = nbuf[pl.ds(192 * g, 192), pl.ds(0, few)].reshape(8, 3, 8, few)
+            for q in range(3):
+                plain = tbuf[pl.ds(64 * g, 64), pl.ds(q * few, few)]
+                to = pl.ds(h * half_cols + q * few, few)
+                units[u, g, :, to] = jnp.where(natural[:, :few], turned[:, q].reshape(64, few), plain)
+
     def arrived(ref, sem):
         pltpu.make_async_copy(ref, ref, sem).wait()
 
-    class Early:
-        def __init__(self, k):
-            self.k, self.sends = k, []
-            self.base = 12 * k
-
-        def group(self, g):
-            return units.at[self.k, :, pl.ds(pl.multiple_of(8 * g, 8), 8)]
-
+    class Chunk:
+        def __init__(self, u, slot, first=0, count=None, away=None):
+            self.u, self.away, self.sends, self.base = u, away, [], 12 * slot
+            self.cut = pl.ds(first, width if count is None else count)
+
+        def go(self, index, src, dst, sem=None, **where):
+            at = self.base + index
+            cp = remote(src, dst, sum_send.at[at], sum_recv.at[at] if sem is None else sem, **where)
+            cp.start()
+            self.sends.append(cp)
+
+        def y_rows(self, g):
+            return units.at[self.u, :, pl.ds(pl.multiple_of(8 * g, 8), 8), self.cut]
+
+        def x_ends(self):
+            for d in range(1, NX):
+                self.go(7 + d, wide.at[self.u, at_x(d), :, self.cut], w_got.at[self.u, d, :, self.cut], x=at_x(d))
+
+        def end(self):
+            total = wide[self.u, x, :, self.cut]
+            for d in range(1, NX):
+                self.sends[-NX + d].wait_recv()
+                total = total + w_got[self.u, d, :, self.cut]
+            res[self.u, :, self.cut] = total
+
+    class RingY(Chunk):
         def slot(self, step, side):
-            return ry_half.at[self.k, side] if step == 0 else ry_full.at[self.k, step - 1, side]
-
-        def out(self, step, srcs):
+            return ry_half.at[self.u, side] if step == 0 else ry_full.at[self.u, step - 1, side]
+
+        def both(self, step, srcs):
             for side in range(2):
-                at = self.base + 2 * step + side
-                cp = remote(
-                    srcs[side], self.slot(step, side), sum_send.at[at], sum_recv.at[at], y=at_y(1 - 2 * side)
-                )
-                cp.start()
-                self.sends.append(cp)
+                self.go(2 * step + side, srcs[side], self.slot(step, side), y=at_y(1 - 2 * side))
 
         def begin(self):
-            far = self.group(at_y(NY // 2))
-            self.out(0, [far.at[pl.ds(2 * side, 2)] for side in range(2)])
+            far = self.y_rows(at_y(NY // 2))
+            self.both(0, [far.at[pl.ds(2 * side, 2)] for side in range(2)])
 
         def middle(self, step):
             last = self.sends[-2:]
             for side in range(2):
                 last[side].wait_recv()
-                where = self.group(at_y((NY // 2 - step) * (1 - 2 * side)))
+                where = self.y_rows(at_y((NY // 2 - step) * (1 - 2 * side)))
                 if step == 1:
                     where = where.at[pl.ds(2 * side, 2)]
                 where[...] = where[...] + self.slot(step - 1, side)[...]
-            self.out(step, [self.group(at_y((NY // 2 - step) * (1 - 2 * side))) for side in range(2)])
+            self.both(step, [self.y_rows(at_y((NY // 2 - step) * (1 - 2 * side))) for side in range(2)])
 
         def across(self):
             for cp in self.sends[-2:]:
                 cp.wait_recv()
             deep = NY // 2 - 1
-            wide[self.k, pl.ds(0, 4)] = self.group(y)[...] + self.slot(deep, 0)[...] + self.slot(deep, 1)[...]
-            for d in range(1, NX):
-                at = self.base + 7 + d
-                cp = remote(
-                    wide.at[self.k, at_x(d)], w_got.at[self.k, d], sum_send.at[at], sum_recv.at[at], x=at_x(d)
-                )
-                cp.start()
-                self.sends.append(cp)
-
-        def end(self):
-            total = wide[self.k, x]
-            for d in range(1, NX):
-                self.sends[-NX + d].wait_recv()
-                total = total + w_got[self.k, d]
-            res[self.k] = total
-
-    class Late:
-        def __init__(self, k, away):
-            self.k, self.u, self.away, self.sends = k, 3 + k, away, []
-            self.base = 12 * self.u
-
+            wide[self.u, pl.ds(0, 4)] = self.y_rows(y)[...] + self.slot(deep, 0)[...] + self.slot(deep, 1)[...]
+            self.x_ends()
+
+    class AllX(Chunk):
         def begin(self):
             for d in (2, 1, 3):
-                at = self.base + d
-                cp = remote(
-                    units.at[self.u, at_x(d)], rx_got.at[self.k, d - 1], sum_send.at[at], sum_recv.at[at], x=at_x(d)
+                self.go(
+                    d, units.at[self.u, at_x(d), :, self.cut], rx_got.at[self.u, d - 1, :, self.cut], x=at_x(d)
                 )
-                cp.start()
-                self.sends.append(cp)
 
         def across(self):
-            total = units[self.u, x]
+            total = units[self.u, x, :, self.cut]
             for i, d in enumerate((2, 1, 3)):
                 self.sends[i].wait_recv()
-                total = total + rx_got[self.k, d - 1]
-            wide[self.u] = total.reshape(8, 8, width)
-            for d in (4, 3, 5, 2, 6, 1, 7, 0):
-                at = self.base + 4 + d
-                if self.away:
-                    cp = remote(
-                        wide.at[self.u, at_y(d)], w_got.at[self.k, d], sum_send.at[at], own_recv.at[8 * self.k + d],
-                        z=z_up, c=0, y=at_y(d),
-                    )
-                elif d:
-                    cp = remote(
-                        wide.at[self.u, at_y(d)], w_got.at[self.u, d], sum_send.at[at], sum_recv.at[at], y=at_y(d)
-                    )
+                total = total + rx_got[self.u, d - 1, :, self.cut]
+            wide[self.u, :, :, self.cut] = total.reshape(8, 8, -1)
+            for d in FAR_FIRST + ((0,) if self.away is not None else ()):
+                src, dst = wide.at[self.u, at_y(d), :, self.cut], w_got.at[self.u, d, :, self.cut]
+                if self.away is None:
+                    self.go(4 + d, src, dst, y=at_y(d))
                 else:
-                    continue
-                cp.start()
-                self.sends.append(cp)
+                    self.go(4 + d, src, dst, own_recv.at[8 * self.away + d], z=z_up, c=0, y=at_y(d))
 
         def end(self):
-            total = wide[self.u, y]
-            for i, d in enumerate((4, 3, 5, 2, 6, 1, 7)):
+            total = wide[self.u, y, :, self.cut]
+            for i, d in enumerate(FAR_FIRST):
                 self.sends[3 + i].wait_recv()
-                total = total + w_got[self.u, d]
-            res[self.u] = total
-
-    def end_c(k):
+                total = total + w_got[self.u, d, :, self.cut]
+            res[self.u, :, self.cut] = total
+
+    def end_c(k, away, first=0, count=None):
         total = None
+        cut = pl.ds(first, width if count is None else count)
         for d in range(NY):
-            arrived(w_got.at[k, d], own_recv.at[8 * k + d])
-            total = w_got[k, d] if total is None else total + w_got[k, d]
-        res[k] = total
-
-    def finish_tile(direct, turned):
+            arrived(w_got.at[3 + k, d, :, cut], own_recv.at[8 * away + d])
+            total = w_got[3 + k, d, :, cut] if total is None else total + w_got[3 + k, d, :, cut]
+        res[3 + k, :, cut] = total
+
+    def put_back(piece, k):
+        top = piece.astype(BF16).astype(F32)
+        rest = piece - top
+        mid = rest.astype(BF16).astype(F32)
+        stack = jnp.concatenate([top, mid, rest - mid], axis=0).astype(BF16)
+        total = jnp.dot(stack, shift[k], preferred_element_type=F32)
+        return total[:24] + total[24:48] + total[48:]
+
+    def finish_early(direct, turned):
         total = None
-        for k in range(3):
-            out[0, pl.ds(8 * k, 8), :] = direct(k)
+        for k in range(2):
             piece = turned(k)
             piece = jnp.concatenate([piece[:, q * cols : (q + 1) * cols] for q in range(3)], axis=0)
-            top = piece.astype(BF16).astype(F32)
-            rest = piece - top
-            mid = rest.astype(BF16).astype(F32)
-            stack = jnp.concatenate([top, mid, rest - mid], axis=0).astype(BF16)
-            term = jnp.dot(stack, shift[k], preferred_element_type=F32)
+            term = put_back(piece, k)
             total = term if total is None else total + term
-        value = out[0] + (total[:24] + total[24:48] + total[48:])
+        out[0] = total
+        for k in range(2):
+            out[0, pl.ds(8 * k, 8), :] = out[0, pl.ds(8 * k, 8), :] + direct(k)
         mine, other = scale[0], scale[1]
         left = jnp.where(own_first, mine, other)
         right = jnp.where(own_first, other, mine)
         i = lax.broadcasted_iota(jnp.int32, (24, width), 0)
         j = lax.broadcasted_iota(jnp.int32, (24, width), 1)
         down = jnp.sum(jnp.where(j == i + 24 * t, left, F32(0)), axis=1, keepdims=True)
-        out[0] = value * down * right
+        both[...] = down * right
+
+    def finish(direct, turned):
+        few, half_cols = cols // 2, width // 2
+        piece = turned(2)
+        piece = jnp.concatenate(
+            [
+                jnp.concatenate([piece[:, h * half_cols + q * few : h * half_cols + (q + 1) * few] for q in range(3)], axis=0)
+                for h in range(2)
+            ],
+            axis=1,
+        )
+        value = out[0] + put_back(piece, 2)
+        straight = direct(2)
+        low_half, high_half = straight[:, :half_cols], straight[:, half_cols:]
+        top = lax.broadcasted_iota(jnp.int32, (8, half_cols), 0) < 4
+        straight = jnp.concatenate(
+            [
+                jnp.where(top, low_half, pltpu.roll(high_half, 4, 0)),
+                jnp.where(top, pltpu.roll(low_half, 4, 0), high_half),
+            ],
+            axis=1,
+        )
+        out[0, pl.ds(0, 16), :] = value[:16] * both[pl.ds(0, 16), :]
+        out[0, pl.ds(16, 8), :] = (value[16:] + straight) * both[pl.ds(16, 8), :]
 
     def wait_sends(*groups):
         for group in groups:
             for cp in group:
                 cp.wait_send()
 
+    whole, halves = pl.ds(0, cols), [pl.ds(cols // 2 * h, cols // 2) for h in range(2)]
+    pieces = [(0, whole), (1, whole), (2, halves[0]), (2, halves[1])]
+    half_width = width // 2
     nothing = jnp.zeros((8, width), F32)
     first_rows, last_rows = pl.ds(0, half), pl.ds(half, half)
 
     @pl.when(c == 0)
     def _():
         flags = remote(flag, flag_c, f_send, f_recv, z=z_down, c=1)
-        to_c = [remote(sent.at[k, 1], got_c.at[k], z_send.at[k], z_recv.at[k], z=z_down, c=1) for k in range(3)]
+        to_c = [
+            remote(sent.at[k, 1, r], got_c.at[k, r], z_send.at[i], z_recv.at[i], z=z_down, c=1)
+            for i, (k, r) in enumerate(pieces)
+        ]
         to_a = [
             [remote(sent.at[k, h], got.at[k, h], core_send.at[k, h], a_recv.at[k, h], c=1) for h in range(2)]
             for k in range(3)
@@ -317,42 +361,66 @@
             if k:
                 chunk(k, 1)
                 to_c[k].start()
+                if k == 2:
+                    to_c[3].start()
                 to_a[k][1].start()
             chunk(k, 0)
             to_a[k][0].start()
         total = masks(0, half, [(nat, 0, jnp.maximum(onsets[own], onsets[low]))], nothing)
         norm_x(masks(half, rows, [], total))
 
-        tiles = [Late(k, False) for k in range(3)]
+        tiles = [RingY(0, 0), RingY(1, 1)]
+        last = [AllX(2, 2, 0, half_width), AllX(2, 6, half_width, half_width)]
 
         def make(k):
             arrived(got.at[k, 0], z_recv.at[k])
-            product(3 + k, ((got.at[k, 0], nat.at[first_rows]),), own_first)
+            product(k, ((got.at[k, 0], nat.at[first_rows]),), own_first)
             tiles[k].begin()
+
+        def make_last(h):
+            moved = got.at[2, 0, halves[h]]
+            arrived(moved, z_recv.at[2 + h])
+            product_half(2, h, ((moved, nat.at[first_rows]),), jnp.broadcast_to(own_first, (64, cols)))
+            last[h].begin()
 
         make(0)
         norm_y()
+        tiles[0].middle(1)
         make(1)
+        tiles[0].middle(2)
+        norm_end(passed)
+        tiles[1].middle(1)
+        make_last(0)
+        make_last(1)
+        tiles[0].middle(3)
+        tiles[1].middle(2)
+        last[0].across()
         tiles[0].across()
-        norm_end(passed)
-        make(2)
+        tiles[1].middle(3)
+        last[1].across()
+        tiles[0].end()
+        end_c(0, 0)
         tiles[1].across()
-        tiles[0].end()
-        end_c(0)
-        tiles[2].across()
+        wait_sends([flags, passed], to_c, nx, ny, *to_a, tiles[0].sends)
+        arrived(scale.at[1], n_recv.at[10])
+        end_c(1, 1)
         tiles[1].end()
-        end_c(1)
-        tiles[2].end()
-        end_c(2)
-        arrived(scale.at[1], n_recv.at[10])
-        finish_tile(
-            lambda k: jnp.where(own_first, res[k], res[3 + k]), lambda k: jnp.where(own_first, res[3 + k], res[k])
-        )
-        wait_sends([flags, passed], to_c, nx, ny, *to_a, *(tile.sends for tile in tiles))
+        direct = lambda k: jnp.where(own_first, res[3 + k], res[k])
+        turned = lambda k: jnp.where(own_first, res[k], res[3 + k])
+        finish_early(direct, turned)
+        wait_sends(tiles[1].sends)
+        for h in range(2):
+            last[h].end()
+            end_c(2, 2 + h, half_width * h, half_width)
+        finish(direct, turned)
+        wait_sends(last[0].sends, last[1].sends)
 
     @pl.when(c == 1)
     def _():
-        to_b = [remote(sent.at[k, 0], got.at[k, 0], z_send.at[k], z_recv.at[k], z=z_up, c=0) for k in range(3)]
+        to_b = [
+            remote(sent.at[k, 0, r], got.at[k, 0, r], z_send.at[i], z_recv.at[i], z=z_up, c=0)
+            for i, (k, r) in enumerate(pieces)
+        ]
         passed = remote(scale.at[0], scale.at[1], n_send.at[10], n_recv.at[10], z=z_up, c=0)
         for i in (0, 1):
             loads[i].wait()
@@ -362,6 +430,7 @@
         for k in (1, 2):
             chunk(k, 0)
             to_b[k].start()
+        to_b[3].start()
         for i in (2, 3):
             loads[i].wait()
         onset_a = jnp.maximum(onsets[own], onsets[low])
@@ -369,48 +438,69 @@
         total = masks(0, half, [(nat, 0, onset_a)], nothing)
         norm_x(masks(half, rows, [(nat, 0, onset_a), (nat_c, half, onset_c)], total))
 
-        early = [Early(k) for k in range(3)]
-        late = [Late(k, True) for k in range(3)]
+        early = [AllX(0, 0), RingY(1, 1), RingY(2, 2)]
+        late = [AllX(3, 3, away=0), AllX(4, 4, away=1)]
+        last = [AllX(5, 5, 0, half_width, 2), AllX(5, 7, half_width, half_width, 3)]
 
         def make_a(k):
             for h in range(2):
                 arrived(got.at[k, h], a_recv.at[k, h])
-            product(k, ((got.at[k, 0], nat.at[first_rows]), (got.at[k, 1], nat.at[last_rows])), own_first)
+            if k < 2:
+                product(k, ((got.at[k, 0], nat.at[first_rows]), (got.at[k, 1], nat.at[last_rows])), own_first)
+            else:
+                for h in range(2):
+                    parts = ((got.at[2, 0, halves[h]], nat.at[first_rows]), (got.at[2, 1, halves[h]], nat.at[last_rows]))
+                    product_half(2, h, parts, jnp.broadcast_to(own_first, (64, cols)))
             early[k].begin()
+
+        def natural_c():
+            return jnp.broadcast_to(flag_c[0:1, 0:1] < F32(0.5), (64, cols))
 
         def make_c(k):
             if k == 0:
                 arrived(flag_c, f_recv)
             arrived(got_c.at[k], z_recv.at[k])
-            natural = jnp.broadcast_to(flag_c[0:1, 0:1] < F32(0.5), (64, cols))
-            product(3 + k, ((got_c.at[k], nat_c),), natural)
+            product(3 + k, ((got_c.at[k], nat_c),), natural_c())
             late[k].begin()
 
-        for k in range(3):
-            make_a(k)
+        def make_last(h):
+            moved = got_c.at[2, halves[h]]
+            arrived(moved, z_recv.at[2 + h])
+            product_half(5, h, ((moved, nat_c),), natural_c())
+            last[h].begin()
+
+        make_a(0)
+        make_a(1)
         make_c(0)
+        make_a(2)
         norm_y()
-        for k in range(3):
+        early[0].across()
+        for k in range(1, 3):
             early[k].middle(1)
         make_c(1)
         late[0].across()
         norm_end(passed)
-        for k in range(3):
+        for k in range(1, 3):
             early[k].middle(2)
-        make_c(2)
+        make_last(0)
+        for k in range(1, 3):
+            early[k].middle(3)
         late[1].across()
-        for k in range(3):
-            early[k].middle(3)
-        late[2].across()
-        for k in range(3):
+        make_last(1)
+        last[0].across()
+        for k in range(1, 3):
             early[k].across()
-        for k in range(3):
-            early[k].end()
+        last[1].across()
+        wait_sends([passed], to_b, nx, ny, late[0].sends, late[1].sends)
         arrived(scale.at[1], n_recv.at[10])
-        finish_tile(
-            lambda k: jnp.where(own_first, F32(0), res[k]), lambda k: jnp.where(own_first, res[k], F32(0))
-        )
-        wait_sends([passed], to_b, nx, ny, *(tile.sends for tile in early + late))
+        early[0].end()
+        early[1].end()
+        direct = lambda k: jnp.where(own_first, F32(0), res[k])
+        turned = lambda k: jnp.where(own_first, res[k], F32(0))
+        finish_early(direct, turned)
+        early[2].end()
+        finish(direct, turned)
+        wait_sends(*(tile.sends for tile in early + last))
 
 
 def on_device(greens, pairs, onsets):
@@ -438,12 +528,13 @@
             vmem((cols, width), F32),
             vmem((width, cols), F32),
             vmem((6, NX, 64, width), F32),
-            vmem((3, NX - 1, 64, width), F32),
+            vmem((6, NX - 1, 64, width), F32),
             vmem((3, 2, 2, 8, width), F32),
             vmem((3, 3, 2, 4, 8, width), F32),
             vmem((6, 8, 8, width), F32),
             vmem((6, 8, 8, width), F32),
             vmem((6, 8, width), F32),
+            vmem((24, width), F32),
             vmem((2, 1, width), F32),
             vmem((NX - 1, 1, width), F32),
             vmem((NY - 1, 1, width), F32),
@@ -451,13 +542,13 @@
             vmem((8, 128), F32),
             vmem((8, 128), F32),
             dma((4,)),
-            dma((3,)),
-            dma((3,)),
+            dma((4,)),
+            dma((4,)),
             dma((3, 2)),
             dma((3, 2)),
-            dma((72,)),
-            dma((72,)),
-            dma((24,)),
+            dma((96,)),
+            dma((96,)),
+            dma((32,)),
             dma((11,)),
             dma((11,)),
             dma,

time: 64.1 us -> 61.2 us (0.955)
  the two profiles are of different devices: /device:TPU:8 before, /device:TPU:2 now
where the time goes in v3:
time: 61.2 us; the launch traced here: 61 us
  Pallas kernels  59.5 us (97%)
  local copies, waits for them, and re-layouts  1.52 us (2%)
    pallas_call x1, Pallas kernels, on_device(): pl.pallas_call(kernel, out_shape=jax.ShapeDtypeStruct((1, width // (NX *...  59.5 us
    unnamed x1, local copies, waits for them, and re-layouts  1.52 us

profile of v3, /device:TPU:2, one launch (start us, length us, event | category | flops | bytes accessed | tf_op | source)
XLA Modules:
  0.0 61.0 jit_solution(4573588959201773520)
XLA Ops:
  0.0 59.5 %shard_map.37 = f32[1,24,768]{2,1,0:T(8,128)} custom-call(bf16[2048,768]{1,0:T(8,128)(2,1)} %greens.1, s32[1,2]{1,0:T(1,128)} %pairs.1, s32[16]{0:T(128)} %onsets.1), custom_call_target="tpu_custom_call" | custom-call | flops 5000000000 | bytes 4000000 | tf_op jit(solution)/shard_map/pallas_call | solution.py:511
  59.5 1.5 %copy.5 = f32[1,24,768]{2,1,0:T(8,128)} copy(f32[1,24,768]{2,1,0:T(8,128)} %shard_map.37) | data formatting | bytes 147456

commit v4 on v3

--- a/solution.py
+++ b/solution.py
@@ -388,10 +388,10 @@
         tiles[0].middle(1)
         make(1)
         tiles[0].middle(2)
+        make_last(0)
+        tiles[1].middle(1)
+        make_last(1)
         norm_end(passed)
-        tiles[1].middle(1)
-        make_last(0)
-        make_last(1)
         tiles[0].middle(3)
         tiles[1].middle(2)
         last[0].across()
@@ -479,18 +479,18 @@
             early[k].middle(1)
         make_c(1)
         late[0].across()
-        norm_end(passed)
+        make_last(0)
         for k in range(1, 3):
             early[k].middle(2)
-        make_last(0)
+        make_last(1)
+        late[1].across()
+        norm_end(passed)
+        last[0].across()
         for k in range(1, 3):
             early[k].middle(3)
-        late[1].across()
-        make_last(1)
-        last[0].across()
+        last[1].across()
         for k in range(1, 3):
             early[k].across()
-        last[1].across()
         wait_sends([passed], to_b, nx, ny, late[0].sends, late[1].sends)
         arrived(scale.at[1], n_recv.at[10])
         early[0].end()

time: 61.2 us -> 60.3 us (0.985)
  the two profiles are of different devices: /device:TPU:2 before, /device:TPU:24 now
where the time goes in v4:
time: 60.3 us; the launch traced here: 60.2 us
  Pallas kernels  58.6 us (97%)
  local copies, waits for them, and re-layouts  1.52 us (3%)
    pallas_call x1, Pallas kernels, on_device(): pl.pallas_call(kernel, out_shape=jax.ShapeDtypeStruct((1, width // (NX *...  58.6 us
    unnamed x1, local copies, waits for them, and re-layouts  1.52 us

profile of v4, /device:TPU:24, one launch (start us, length us, event | category | flops | bytes accessed | tf_op | source)
XLA Modules:
  0.0 60.2 jit_solution(1761511755385598940)
XLA Ops:
  0.0 58.6 %shard_map.37 = f32[1,24,768]{2,1,0:T(8,128)} custom-call(bf16[2048,768]{1,0:T(8,128)(2,1)} %greens.1, s32[1,2]{1,0:T(1,128)} %pairs.1, s32[16]{0:T(128)} %onsets.1), custom_call_target="tpu_custom_call" | custom-call | flops 5000000000 | bytes 4000000 | tf_op jit(solution)/shard_map/pallas_call | solution.py:511
  58.7 1.5 %copy.5 = f32[1,24,768]{2,1,0:T(8,128)} copy(f32[1,24,768]{2,1,0:T(8,128)} %shard_map.37) | data formatting | bytes 147456

commit v5 on v4

--- a/solution.py
+++ b/solution.py
@@ -387,10 +387,10 @@
         norm_y()
         tiles[0].middle(1)
         make(1)
+        make_last(0)
         tiles[0].middle(2)
-        make_last(0)
+        make_last(1)
         tiles[1].middle(1)
-        make_last(1)
         norm_end(passed)
         tiles[0].middle(3)
         tiles[1].middle(2)
@@ -474,15 +474,15 @@
         make_c(0)
         make_a(2)
         norm_y()
+        early[1].middle(1)
         early[0].across()
-        for k in range(1, 3):
-            early[k].middle(1)
         make_c(1)
+        early[2].middle(1)
+        make_last(0)
         late[0].across()
-        make_last(0)
-        for k in range(1, 3):
-            early[k].middle(2)
+        early[1].middle(2)
         make_last(1)
+        early[2].middle(2)
         late[1].across()
         norm_end(passed)
         last[0].across()

time: 60.3 us -> 61.7 us (1.023)
  Pallas kernels: 58.6 us -> 60 us
    pallas_call x1, Pallas kernels: 58.6 us -> 60 us  [on_device(): pl.pallas_call(kernel, out_shape=jax.ShapeDtypeStruct((1, width // (NX *...]
where the time goes in v5:
time: 61.7 us; the launch traced here: 61.6 us
  Pallas kernels  60 us (97%)
  local copies, waits for them, and re-layouts  1.52 us (2%)
    pallas_call x1, Pallas kernels, on_device(): pl.pallas_call(kernel, out_shape=jax.ShapeDtypeStruct((1, width // (NX *...  60 us
    unnamed x1, local copies, waits for them, and re-layouts  1.52 us

profile of v5, /device:TPU:24, one launch (start us, length us, event | category | flops | bytes accessed | tf_op | source)
XLA Modules:
  0.0 61.6 jit_solution(8071260455556223054)
XLA Ops:
  0.0 60.0 %shard_map.37 = f32[1,24,768]{2,1,0:T(8,128)} custom-call(bf16[2048,768]{1,0:T(8,128)(2,1)} %greens.1, s32[1,2]{1,0:T(1,128)} %pairs.1, s32[16]{0:T(128)} %onsets.1), custom_call_target="tpu_custom_call" | custom-call | flops 5000000000 | bytes 4000000 | tf_op jit(solution)/shard_map/pallas_call | solution.py:511
  60.0 1.5 %copy.5 = f32[1,24,768]{2,1,0:T(8,128)} copy(f32[1,24,768]{2,1,0:T(8,128)} %shard_map.37) | data formatting | bytes 147456
